TPU v7x, 32 devices: a whole 2x2x4 slice. The times are simulated.
32 devices in a mesh: dp: 16 (over z, x, core), seq: 2 (over y).
Axes of the slice: x: 2, y: 2, z: 4, core: 2. Of those that a mesh axis runs over, the one named last changes fastest.
Arguments:
- hidden_in: bfloat16 [16384, 2048], P(('dp', 'seq')), may hold values from -6 to 6
- norm_gain: float32 [2048], replicated, may hold values from 0.1 to 1.9
- w_qk: bfloat16 [2048, 3072], P(('dp', 'seq')), may hold values from -1 to 1
- w_v: bfloat16 [2048, 1024], P(('dp', 'seq')), may hold values from -0.125 to 0.125
- w_o: bfloat16 [2048, 2048], P(('dp', 'seq')), may hold values from -0.125 to 0.125
- prompt_pages: int32 [16], replicated, may hold values from 1 to 17, 128 in all
- last_fill: int32 [16], replicated, may hold values from 1 to 128
- page_slots: int32 [128], P('dp'), may hold values from 0 to 7, as said below
Outputs:
- attended: bfloat16 [16384, 2048], P(('dp', 'seq'))
- key_cache: bfloat16 [128, 128, 1024], P(('dp', 'seq'))
- value_cache: bfloat16 [128, 128, 1024], P(('dp', 'seq'))
Inputs may be any that keep to these rules, and one draw needn't show every extreme that they name: `prompt_pages`: the prompts' pages lie end to end from position 0 and add up to 128. `page_slots`: each aligned run of 8 entries is a permutation of 0 to 7.
All inputs are finite; a program needn't handle non-finite values.
Results may differ from a plain program's by a relative error of at most 0.01.
The roundings to bfloat16 on the way count: a program that leaves them out, or rounds other values in their place, can miss the bound.
Values may be sent and summed in bfloat16 or wider, within the bound.
A program may use at most 192 MiB of HBM per device.

v0:
```python
import math

import jax
import jax.numpy as jnp
from jax import lax
from jax.sharding import PartitionSpec as P

HEADS = 16
KV_HEADS = 8
HEAD_DIM = 128
PAGE = 128
REACH = 4


THETA = 1000000.0
EPS = 1e-05
NEG = -1e30


def shifted(block, axis, distance):
    devices = range(lax.axis_size(axis))
    route = [(i - distance, i) for i in devices if i - distance in devices]
    return lax.ppermute(block, axis, route)


def token_tables(prompt_pages, last_fill):
    ends = jnp.cumsum(prompt_pages) * PAGE
    starts = ends - prompt_pages * PAGE
    lengths = (prompt_pages - 1) * PAGE + last_fill
    return (starts, lengths)


def locate(token_ids, starts, lengths):
    inside = (token_ids[:, None] >= starts[None, :]).astype(jnp.int32)
    request = jnp.sum(inside, axis=1) - 1
    match = jnp.arange(starts.shape[0], dtype=jnp.int32)[None, :] == request[:, None]
    start = jnp.sum(jnp.where(match, starts[None, :], 0), axis=1)
    length = jnp.sum(jnp.where(match, lengths[None, :], 0), axis=1)
    position = token_ids - start
    valid = (position < length) & (token_ids >= 0)
    return (request, position, valid)


def pair_mask(query_ids, key_ids, starts, lengths):
    query_req, _, query_valid = locate(query_ids, starts, lengths)
    key_req, _, key_valid = locate(key_ids, starts, lengths)
    allowed = (query_req[:, None] == key_req[None, :]) & (key_ids[None, :] <= query_ids[:, None])
    return allowed & query_valid[:, None] & key_valid[None, :]


def rotate(heads, position):
    half = heads.shape[-1] // 2
    freq = jnp.power(THETA, -2.0 * jnp.arange(half, dtype=jnp.float32) / heads.shape[-1])
    angle = position.astype(jnp.float32)[:, None] * freq[None, :]
    cosine = jnp.concatenate([jnp.cos(angle), jnp.cos(angle)], axis=-1)[:, None, :]
    sine = jnp.concatenate([jnp.sin(angle), jnp.sin(angle)], axis=-1)[:, None, :]
    turned = jnp.concatenate([-heads[..., half:], heads[..., :half]], axis=-1)
    return heads * cosine + turned * sine


def normalize(hidden_in, norm_gain):
    values = hidden_in.astype(jnp.float32)
    scale = lax.rsqrt(jnp.mean(values * values, axis=-1, keepdims=True) + EPS)
    return (values * scale * norm_gain[None, :]).astype(jnp.bfloat16)


def split_heads(projected, value_part, position):
    count = projected.shape[0]
    width = HEADS * HEAD_DIM
    queries = rotate(projected[:, :width].reshape(count, HEADS, HEAD_DIM), position)
    queries = queries.astype(jnp.bfloat16).reshape(count, width)
    keys = rotate(projected[:, width:].reshape(count, KV_HEADS, HEAD_DIM), position)
    keys = keys.astype(jnp.bfloat16).reshape(count, KV_HEADS * HEAD_DIM)
    return (queries, keys, value_part.astype(jnp.bfloat16))


def contract_pair(left, first, second):

    def add_rows(totals, pieces, start):
        return (
            jnp.dot(left, pieces[0], preferred_element_type=jnp.float32),
            jnp.dot(left, pieces[1], preferred_element_type=jnp.float32),
        )

    empty = (
        jnp.zeros((left.shape[0], first.shape[1]), jnp.float32),
        jnp.zeros((left.shape[0], second.shape[1]), jnp.float32),
    )
    return add_rows(
        empty,
        (
            lax.all_gather(first, ("dp", "seq"), axis=0, tiled=True),
            lax.all_gather(second, ("dp", "seq"), axis=0, tiled=True),
        ),
        jnp.int32(0),
    )


def contract_one(left, weight):

    def add_rows(total, piece, start):
        columns = lax.dynamic_slice_in_dim(left, start, piece.shape[0], 1)
        return total + jnp.dot(columns, piece, preferred_element_type=jnp.float32)

    empty = jnp.zeros((left.shape[0], weight.shape[1]), jnp.float32)
    return add_rows(empty, lax.all_gather(weight, ("dp", "seq"), axis=0, tiled=True), jnp.int32(0))


def earlier_blocks(keys, values):
    key_list = [keys]
    value_list = [values]
    for distance in range(1, REACH + 1):
        received = shifted((keys, values), ("dp", "seq"), distance)
        key_list.append(received[0])
        value_list.append(received[1])
    return (jnp.stack(key_list), jnp.stack(value_list))


def attend(queries, key_blocks, value_blocks, masks, valid):
    rows = queries.shape[0]
    group = HEADS // KV_HEADS
    count = key_blocks.shape[0]
    scale = 1.0 / math.sqrt(HEAD_DIM)
    query_heads = queries.reshape(rows, KV_HEADS, group, HEAD_DIM).transpose(1, 0, 2, 3)
    key_heads = key_blocks.reshape(count, rows, KV_HEADS, HEAD_DIM).transpose(2, 0, 1, 3)
    value_heads = value_blocks.reshape(count, rows, KV_HEADS, HEAD_DIM).transpose(2, 0, 1, 3)

    def one_head(operands):
        query_one, key_one, value_one = operands
        score_list = []
        for index in range(count):
            scores_raw = (
                jnp.einsum(
                    "qgd,sd->gqs", query_one, key_one[index], preferred_element_type=jnp.float32
                )
                * scale
            )
            score_list.append(jnp.where(masks[index][None], scores_raw, NEG))
        top = jnp.full((group, rows), NEG, jnp.float32)
        for index in range(count):
            top = jnp.maximum(top, jnp.max(score_list[index], axis=2))
        carry = (
            jnp.zeros((group, rows), jnp.float32),
            jnp.zeros((group, rows, HEAD_DIM), jnp.float32),
        )
        for index in range(count):
            raw = score_list[index]
            block_total, block_numer = carry
            expo = jnp.where(masks[index][None], jnp.exp(raw - top[:, :, None]), 0.0)
            weights = expo.astype(jnp.bfloat16)
            product = jnp.einsum(
                "gqs,sd->gqd", weights, value_one[index], preferred_element_type=jnp.float32
            )
            carry = (block_total + jnp.sum(expo, axis=2), block_numer + product)
        total, numer = carry
        safe = jnp.where(valid[None, :], total, 1.0)
        return jnp.where(valid[None, :, None], numer / safe[:, :, None], 0.0)

    heads = lax.map(one_head, (query_heads, key_heads, value_heads))
    return heads.transpose(2, 0, 1, 3).reshape(rows, HEADS * HEAD_DIM).astype(jnp.bfloat16)


def write_pages(kept_keys, kept_values, page_slots):
    rows = kept_keys.shape[0]
    width = kept_keys.shape[1]
    pages = rows // PAGE
    owners = page_slots.shape[0] // pages
    seq_index = lax.axis_index("seq")
    targets = lax.dynamic_slice_in_dim(page_slots, seq_index * pages, pages)
    owner = targets // pages
    slot = targets % pages
    owner_hit = owner[None, None, :] == jnp.arange(owners, dtype=jnp.int32)[:, None, None]
    slot_hit = slot[None, None, :] == jnp.arange(pages, dtype=jnp.int32)[None, :, None]
    select = (owner_hit & slot_hit).astype(jnp.bfloat16)
    key_send = jnp.einsum(
        "osj,jrc->osrc",
        select,
        kept_keys.reshape(pages, PAGE, width),
        preferred_element_type=jnp.float32,
    ).astype(jnp.bfloat16)
    value_send = jnp.einsum(
        "osj,jrc->osrc",
        select,
        kept_values.reshape(pages, PAGE, width),
        preferred_element_type=jnp.float32,
    ).astype(jnp.bfloat16)
    received = (
        lax.all_to_all(key_send, "seq", split_axis=0, concat_axis=0, tiled=True),
        lax.all_to_all(value_send, "seq", split_axis=0, concat_axis=0, tiled=True),
    )
    return (jnp.sum(received[0], axis=0), jnp.sum(received[1], axis=0))


def shards(hidden_in, norm_gain, w_qk, w_v, w_o, prompt_pages, last_fill, page_slots):
    rows = hidden_in.shape[0]
    device = lax.axis_index("dp") * lax.axis_size("seq") + lax.axis_index("seq")
    starts, lengths = token_tables(prompt_pages, last_fill)
    own_ids = device * rows + jnp.arange(rows, dtype=jnp.int32)
    _, position, valid = locate(own_ids, starts, lengths)
    normed = normalize(hidden_in, norm_gain)
    projected, value_part = contract_pair(normed, w_qk, w_v)
    queries, keys, values = split_heads(projected, value_part, position)
    key_blocks, value_blocks = earlier_blocks(keys, values)
    mask_list = []
    for distance in range(REACH + 1):
        key_ids = (device - distance) * rows + jnp.arange(rows, dtype=jnp.int32)
        mask_list.append(pair_mask(own_ids, key_ids, starts, lengths))
    masks = jnp.stack(mask_list)
    attn = attend(queries, key_blocks, value_blocks, masks, valid)
    attended = contract_one(attn, w_o).astype(jnp.bfloat16)
    kept_keys = jnp.where(valid[:, None], keys, jnp.zeros_like(keys))
    kept_values = jnp.where(valid[:, None], values, jnp.zeros_like(values))
    key_cache, value_cache = write_pages(kept_keys, kept_values, page_slots)
    return (attended, key_cache, value_cache)


def solution(mesh):
    in_specs = (
        P(("dp", "seq"), None),
        P(),
        P(("dp", "seq"), None),
        P(("dp", "seq"), None),
        P(("dp", "seq"), None),
        P(),
        P(),
        P("dp"),
    )
    out_specs = (P(("dp", "seq"), None), P(("dp", "seq"), None, None), P(("dp", "seq"), None, None))
    return jax.shard_map(shards, mesh=mesh, in_specs=in_specs, out_specs=out_specs, check_vma=False)
```

profile of v0, /device:TPU:13, one launch (start us, length us, event | category | flops | bytes accessed | tf_op | source)
XLA Modules:
  0.0 611.4 jit_solution(4650662037410422154)
XLA Ops:
  14.9 92.9 %all-gather.4.cloned.1.call-done = bf16[2048,3072]{1,0:T(8,128)(2,1)} async-done(((bf16[64,3072]{1,0:T(8,128)(2,1)}), bf16[2048,3072]{1,0:T(8,128)(2,1)}) %all-gather.4.cloned.1.call-update) | async-done | bytes 12582928 | tf_op jit(solution)/shard_map/all_gather | solution.py:92
  107.9 9.3 %fusion.108 = f32[512,3072]{1,0:T(8,128)S(1)} fusion(bf16[2048,3072]{1,0:T(8,128)(2,1)} %all-gather.4.cloned.1.call-done, bf16[512,2048]{1,0:T(8,128)(2,1)S(1)} %copy-done.9, f32[2048]{0:T(1024)S(1)} %copy-done.14, f32[512]{0:T(512)S(1)} %add_rsqrt_fusion), kind=kOutput, calls=%fused_computation.155 | convolution fusion | flops 6446645248 | bytes 20981760 | tf_op jit(solution)/shard_map/dot_general | solution.py:81
  120.5 3.9 copy_negate_fusion
  124.4 47.2 %all-gather.6.cloned.1.call-done = bf16[2048,1024]{1,0:T(8,128)(2,1)} async-done(((bf16[64,1024]{1,0:T(8,128)(2,1)}), bf16[2048,1024]{1,0:T(8,128)(2,1)}) %all-gather.6.cloned.1.call-update) | async-done | bytes 4194320 | tf_op jit(solution)/shard_map/all_gather | solution.py:93
  173.2 7.8 %broadcast_select_fusion.1 = (bf16[512,1024]{1,0:T(8,128)(2,1)}, bf16[512,1024]{1,0:T(8,128)(2,1)}, bf16[512,1024]{1,0:T(8,128)(2,1)}, bf16[512,1024]{1,0:T(8,128)(2,1)}) fusion(pred[512]{0:T(512)(128)(4,1)S(1)} %compare_and_fusion, f32[64,8,8,128]{3,2,1,0:T(8,128)S(1)} %bitcast.304, f32[512,3072]{1,0:T(8,128)} %copy-done.7, ...), kind=kOutput, calls=%fused_computation.154 | convolution fusion | flops 2155872256 | bytes 17050112 | tf_op jit(solution)/shard_map/dot_general | solution.py:82
  186.4 3.6 collective-permute-start.2
  194.6 5.3 copy.134
  199.9 3.4 collective-permute-start.4
  210.3 11.4 %collective-permute-start.5 = (bf16[512,1024]{1,0:T(8,128)(2,1)}, bf16[512,1024]{1,0:T(8,128)(2,1)}, u32[]{:S(2)}, u32[]{:S(2)}) collective-permute-start(bf16[512,1024]{1,0:T(8,128)(2,1)} %get-tuple-element.311), channel_id=1, source_target_pairs={{0,2},{1,3},{2,4},{3,5},{4,6},{5,7},{6,8},{7,9},{8,10},{9,11},{10,... | collective-permute-start | bytes 3145736 | tf_op jit(solution)/shard_map/ppermute | solution.py:23
  221.7 7.2 %collective-permute-done.1 = bf16[512,1024]{1,0:T(8,128)(2,1)} collective-permute-done((bf16[512,1024]{1,0:T(8,128)(2,1)}, bf16[512,1024]{1,0:T(8,128)(2,1)}, u32[]{:S(2)}, u32[]{:S(2)}) %collective-permute-start.1) | collective-permute-done | bytes 1048608 | tf_op jit(solution)/shard_map/ppermute | solution.py:23
  230.8 24.8 %collective-permute-done.2 = bf16[512,1024]{1,0:T(8,128)(2,1)} collective-permute-done((bf16[512,1024]{1,0:T(8,128)(2,1)}, bf16[512,1024]{1,0:T(8,128)(2,1)}, u32[]{:S(2)}, u32[]{:S(2)}) %collective-permute-start.2) | collective-permute-done | bytes 1048608 | tf_op jit(solution)/shard_map/ppermute | solution.py:23
  255.6 25.4 %collective-permute-start.7 = (bf16[512,1024]{1,0:T(8,128)(2,1)}, bf16[512,1024]{1,0:T(8,128)(2,1)}, u32[]{:S(2)}, u32[]{:S(2)}) collective-permute-start(bf16[512,1024]{1,0:T(8,128)(2,1)} %get-tuple-element.311), channel_id=1, source_target_pairs={{0,4},{1,5},{2,6},{3,7},{4,8},{5,9},{6,10},{7,11},{8,12},{9,13},{1... | collective-permute-start | bytes 3145736 | tf_op jit(solution)/shard_map/ppermute | solution.py:23
  282.1 6.6 %reshape.1064 = f32[512,8,2,128]{3,2,1,0:T(2,128)} reshape(f32[512,2048]{1,0:T(8,128)} %slice.87) | data formatting | bytes 8388608 | tf_op jit(solution)/shard_map/reshape | solution.py:70
  288.7 3.9 copy.136
  292.6 3.8 copy.135
  296.4 6.1 %all-to-all-start = ((bf16[2,4,128,1024]{3,1,2,0:T(4,128)(2,1)}), bf16[2,4,128,1024]{3,1,2,0:T(4,128)(2,1)}, u32[]{:S(2)}, u32[]{:S(2)}) async-start(bf16[2,4,128,1024]{3,1,2,0:T(4,128)(2,1)} %convolution_convert_fusion.2), calls=%async_computation | async-start | bytes 4194304 | tf_op jit(solution)/shard_map/all_to_all | solution.py:188
  302.6 4.0 convolution_convert_fusion.1
  309.4 5.5 fusion.96
  323.9 7.0 %collective-permute-done.6 = bf16[512,1024]{1,0:T(8,128)(2,1)} collective-permute-done((bf16[512,1024]{1,0:T(8,128)(2,1)}, bf16[512,1024]{1,0:T(8,128)(2,1)}, u32[]{:S(2)}, u32[]{:S(2)}) %collective-permute-start.6) | collective-permute-done | bytes 1048608 | tf_op jit(solution)/shard_map/ppermute | solution.py:23
  332.4 26.7 %collective-permute-done.7 = bf16[512,1024]{1,0:T(8,128)(2,1)} collective-permute-done((bf16[512,1024]{1,0:T(8,128)(2,1)}, bf16[512,1024]{1,0:T(8,128)(2,1)}, u32[]{:S(2)}, u32[]{:S(2)}) %collective-permute-start.7) | collective-permute-done | bytes 1048608 | tf_op jit(solution)/shard_map/ppermute | solution.py:23
  366.9 5.0 all-to-all-start.1
  371.9 214.5 %while.12 = (s32[]{:T(128)}, bf16[8,2,512,128]{2,3,1,0:T(8,128)(2,1)}, pred[512]{0:T(512)(128)(4,1)S(1)}, bf16[8,5,512,128]{3,2,1,0:T(8,128)(2,1)}, bf16[8,512,2...) while((s32[]{:T(128)}, ...), condition=%wide.region_28.29_spmd.clone.clone, body=%wide.region_17.28_spmd.clone.clone.sunk | while | flops 1383596032 | bytes 70142872 | solution.py:159
  591.1 3.4 reduce_sum.240
  595.8 9.1 %convolution_convert_fusion = bf16[512,2048]{1,0:T(8,128)(2,1)} fusion(bf16[512,2048]{0,1:T(8,128)(2,1)S(1)} %bitcast.308, bf16[2048,2048]{1,0:T(8,128)(2,1)} %all-gather.8.cloned.1.call-done), kind=kOutput, calls=%fused_computation.122 | convolution fusion | flops 4296015872 | bytes 12582912 | tf_op jit(solution)/shard_map/dot_general | solution.py:103
  (282 shorter events, 272.7 us)
Async XLA Ops:
  7.2 100.7 %all-gather.4.cloned.1.call-start = ((), (), s32[]{:S(2)}) async-start(), calls=%async_computation.2 | async-start | bytes 12976128 | tf_op jit(solution)/shard_map/all_gather | solution.py:92
  7.9 163.7 %all-gather.6.cloned.1.call-start = ((), (), s32[]{:S(2)}) async-start(), calls=%async_computation.3 | async-start | bytes 4325376 | tf_op jit(solution)/shard_map/all_gather | solution.py:93
  8.6 6.1 %copy-start.12 = (s32[8]{0:T(128)S(1)}, s32[8]{0:T(128)}, u32[]{:S(2)}) copy-start(s32[8]{0:T(128)} %param.17) | copy-start | bytes 100
  8.7 99.2 %copy-start.9 = (bf16[512,2048]{1,0:T(8,128)(2,1)S(1)}, bf16[512,2048]{1,0:T(8,128)(2,1)}, u32[]{:S(2)}) copy-start(bf16[512,2048]{1,0:T(8,128)(2,1)} %param.10) | copy-start | bytes 6291460
  8.7 99.2 %copy-start.14 = (f32[2048]{0:T(1024)S(1)}, f32[2048]{0:T(1024)}, u32[]{:S(2)}) copy-start(f32[2048]{0:T(1024)} %param.11) | copy-start | bytes 24580
  8.7 587.1 %all-gather.8.cloned.1.call-start = ((), (), s32[]{:S(2)}) async-start(), calls=%async_computation.4 | async-start | bytes 8650752 | tf_op jit(solution)/shard_map/all_gather | solution.py:106
  171.8 20.5 %slice-start = ((s8[6291456]{0:T(1024)(128)(4,1)}), s8[4194304]{0:T(1024)(128)(4,1)S(1)}, s32[]{:S(2)}) async-start(s8[6291456]{0:T(1024)(128)(4,1)} %bitcast.292), calls=%async_computation.5 | async-start | bytes 8388608
  173.2 19.0 %slice-start.1 = ((s8[6291456]{0:T(1024)(128)(4,1)}), s8[2097152]{0:T(1024)(128)(4,1)S(1)}, s32[]{:S(2)}) async-start(s8[6291456]{0:T(1024)(128)(4,1)} %bitcast.292), calls=%async_computation.6 | async-start | bytes 4194304
  181.0 29.3 %collective-permute-start = (bf16[512,1024]{1,0:T(8,128)(2,1)}, bf16[512,1024]{1,0:T(8,128)(2,1)}, u32[]{:S(2)}, u32[]{:S(2)}) collective-permute-start(bf16[512,1024]{1,0:T(8,128)(2,1)} %get-tuple-element.282), channel_id=1, source_target_pairs={{0,1},{1,2},{2,3},{3,4},{4,5},{5,6},{6,7},{7,8},{8,9},{9,10},{10,1... | collective-permute-start | bytes 3145736 | tf_op jit(solution)/shard_map/ppermute | solution.py:23
  184.0 44.9 %collective-permute-start.1 = (bf16[512,1024]{1,0:T(8,128)(2,1)}, bf16[512,1024]{1,0:T(8,128)(2,1)}, u32[]{:S(2)}, u32[]{:S(2)}) collective-permute-start(bf16[512,1024]{1,0:T(8,128)(2,1)} %get-tuple-element.282), channel_id=1, source_target_pairs={{0,2},{1,3},{2,4},{3,5},{4,6},{5,7},{6,8},{7,9},{8,10},{9,11},{10,... | collective-permute-start | bytes 3145736 | tf_op jit(solution)/shard_map/ppermute | solution.py:23
  186.4 69.2 %collective-permute-start.2 = (bf16[512,1024]{1,0:T(8,128)(2,1)}, bf16[512,1024]{1,0:T(8,128)(2,1)}, u32[]{:S(2)}, u32[]{:S(2)}) collective-permute-start(bf16[512,1024]{1,0:T(8,128)(2,1)} %get-tuple-element.282), channel_id=1, source_target_pairs={{0,3},{1,4},{2,5},{3,6},{4,7},{5,8},{6,9},{7,10},{8,11},{9,12},{10... | collective-permute-start | bytes 3145736 | tf_op jit(solution)/shard_map/ppermute | solution.py:23
  190.1 129.3 %collective-permute-start.3 = (bf16[512,1024]{1,0:T(8,128)(2,1)}, bf16[512,1024]{1,0:T(8,128)(2,1)}, u32[]{:S(2)}, u32[]{:S(2)}) collective-permute-start(bf16[512,1024]{1,0:T(8,128)(2,1)} %get-tuple-element.282), channel_id=1, source_target_pairs={{0,4},{1,5},{2,6},{3,7},{4,8},{5,9},{6,10},{7,11},{8,12},{9,13},{1... | collective-permute-start | bytes 3145736 | tf_op jit(solution)/shard_map/ppermute | solution.py:23
  199.9 5.1 copy-start.11
  199.9 120.9 %collective-permute-start.4 = (bf16[512,1024]{1,0:T(8,128)(2,1)}, bf16[512,1024]{1,0:T(8,128)(2,1)}, u32[]{:S(2)}, u32[]{:S(2)}) collective-permute-start(bf16[512,1024]{1,0:T(8,128)(2,1)} %get-tuple-element.311), channel_id=1, source_target_pairs={{0,1},{1,2},{2,3},{3,4},{4,5},{5,6},{6,7},{7,8},{8,9},{9,10},{10,1... | collective-permute-start | bytes 3145736 | tf_op jit(solution)/shard_map/ppermute | solution.py:23
  203.3 4.3 copy-start.3
  210.3 112.0 %collective-permute-start.5 = (bf16[512,1024]{1,0:T(8,128)(2,1)}, bf16[512,1024]{1,0:T(8,128)(2,1)}, u32[]{:S(2)}, u32[]{:S(2)}) collective-permute-start(bf16[512,1024]{1,0:T(8,128)(2,1)} %get-tuple-element.311), channel_id=1, source_target_pairs={{0,2},{1,3},{2,4},{3,5},{4,6},{5,7},{6,8},{7,9},{8,10},{9,11},{10,... | collective-permute-start | bytes 3145736 | tf_op jit(solution)/shard_map/ppermute | solution.py:23
  228.9 102.0 %collective-permute-start.6 = (bf16[512,1024]{1,0:T(8,128)(2,1)}, bf16[512,1024]{1,0:T(8,128)(2,1)}, u32[]{:S(2)}, u32[]{:S(2)}) collective-permute-start(bf16[512,1024]{1,0:T(8,128)(2,1)} %get-tuple-element.311), channel_id=1, source_target_pairs={{0,3},{1,4},{2,5},{3,6},{4,7},{5,8},{6,9},{7,10},{8,11},{9,12},{10... | collective-permute-start | bytes 3145736 | tf_op jit(solution)/shard_map/ppermute | solution.py:23
  255.6 103.5 %collective-permute-start.7 = (bf16[512,1024]{1,0:T(8,128)(2,1)}, bf16[512,1024]{1,0:T(8,128)(2,1)}, u32[]{:S(2)}, u32[]{:S(2)}) collective-permute-start(bf16[512,1024]{1,0:T(8,128)(2,1)} %get-tuple-element.311), channel_id=1, source_target_pairs={{0,4},{1,5},{2,6},{3,7},{4,8},{5,9},{6,10},{7,11},{8,12},{9,13},{1... | collective-permute-start | bytes 3145736 | tf_op jit(solution)/shard_map/ppermute | solution.py:23
  296.4 70.5 %all-to-all-start = ((bf16[2,4,128,1024]{3,1,2,0:T(4,128)(2,1)}), bf16[2,4,128,1024]{3,1,2,0:T(4,128)(2,1)}, u32[]{:S(2)}, u32[]{:S(2)}) async-start(bf16[2,4,128,1024]{3,1,2,0:T(4,128)(2,1)} %convolution_convert_fusion.2), calls=%async_computation | async-start | bytes 4194304 | tf_op jit(solution)/shard_map/all_to_all | solution.py:188
  302.6 4.0 copy-start.6
  302.6 6.6 %copy-start.5 = (f32[512,8,2,64]{3,0,2,1:T(8,128)S(1)}, f32[512,8,2,64]{3,0,2,1:T(8,128)}, u32[]{:S(2)}) copy-start(f32[512,8,2,64]{3,0,2,1:T(8,128)} %copy.136) | copy-start | bytes 6291460
  361.7 4.1 copy-start.8
  366.9 224.2 %all-to-all-start.1 = ((bf16[2,4,128,1024]{3,1,2,0:T(4,128)(2,1)}), bf16[2,4,128,1024]{3,1,2,0:T(4,128)(2,1)}, u32[]{:S(2)}, u32[]{:S(2)}) async-start(bf16[2,4,128,1024]{3,1,2,0:T(4,128)(2,1)} %convolution_convert_fusion.1), calls=%async_computation.1 | async-start | bytes 4194304 | tf_op jit(solution)/shard_map/all_to_all | solution.py:189
  591.0 4.7 copy-start.13
  (27 other events, 52.2 us)
Sparse Core Ops, SparseCore 0:
  10.9 96.9 all-gather.3
  110.7 60.8 all-gather.5
  174.7 118.2 all-gather.7
where the time goes:
time: 614 us; the launch traced here: 611 us
  waiting for transfers between devices  208 us (34%)
  matrix products  202 us (33%)
  starting transfers between devices  64.6 us (11%)
  other arithmetic  63.2 us (10%)
  local copies, waits for them, and re-layouts  58.4 us (10%)
  between operations  14.3 us (2%)
    dot_general x40, matrix products, one_head(): jnp.einsum('qgd,sd->gqs', query_one, key_one[index], preferred_element_ty...  95.9 us
    all_gather x1, waiting for transfers between devices, contract_pair(): lax.all_gather(first, ('dp', 'seq'), axis=0, tiled=True)  92.9 us
    dot_general x40, matrix products, one_head(): jnp.einsum('gqs,sd->gqd', weights, value_one[index], preferred_element_ty...  73.4 us
    ppermute x8, waiting for transfers between devices, shifted(): return lax.ppermute(block, axis, route)  65.7 us
    ppermute x8, starting transfers between devices, shifted(): return lax.ppermute(block, axis, route)  53.3 us
    all_gather x1, waiting for transfers between devices, contract_pair(): lax.all_gather(second, ('dp', 'seq'), axis=0, tiled=True)  47.2 us
    unnamed x48, local copies, waits for them, and re-layouts  26.5 us
    reduce_sum x8, other arithmetic, one_head(): carry = (block_total + jnp.sum(expo, axis=2), block_numer + product)  22.6 us
  transfers between devices with their start and end apart: 13, of which 6 were waited for; matrix products, arithmetic and copies ran while one was open for 51% of the time, Pallas kernels for 0%

commit v1 on v0

v1 whole, which is shorter than its diff:
```python
import functools
import math

import jax
import jax.numpy as jnp
from jax import lax
from jax.experimental import pallas as pl
from jax.experimental.pallas import tpu as pltpu
from jax.sharding import Mesh, PartitionSpec as P

HEADS = 16
KV_HEADS = 8
HEAD_DIM = 128
PAGE = 128
GROUP = 4
CHUNK = 4
THETA = 1000000.0
EPS = 1e-05
NEG = -1e30
VMEM = 56 * 1024 * 1024

Q_COLS = HEADS * HEAD_DIM // GROUP
KV_COLS = KV_HEADS * HEAD_DIM // GROUP
KV_PER = KV_HEADS // GROUP
SHARE = HEADS // KV_HEADS


def normalize(hidden_in, norm_gain):
    values = hidden_in.astype(jnp.float32)
    scale = lax.rsqrt(jnp.mean(values * values, axis=-1, keepdims=True) + EPS)
    return (values * scale * norm_gain[None, :]).astype(jnp.bfloat16)


def page_tables(first_page, pages, prompt_pages, last_fill):
    ends = jnp.cumsum(prompt_pages)
    starts = ends - prompt_pages
    ids = first_page + jnp.arange(pages, dtype=jnp.int32)
    mine = (ids[:, None] >= starts[None, :]) & (ids[:, None] < ends[None, :])
    start = jnp.sum(jnp.where(mine, starts[None, :], 0), axis=1)
    end = jnp.sum(jnp.where(mine, ends[None, :], 0), axis=1)
    fill = jnp.sum(jnp.where(mine, last_fill[None, :], 0), axis=1)
    back = ids - start
    live = jnp.where(ids == end - 1, fill, PAGE)
    return back.astype(jnp.int32), live.astype(jnp.int32)


def rope_tables(back, pages):
    half = HEAD_DIM // 2
    position = (back[:, None] * PAGE + jnp.arange(PAGE, dtype=jnp.int32)[None, :]).reshape(pages * PAGE)
    freq = jnp.power(THETA, -2.0 * jnp.arange(half, dtype=jnp.float32) / HEAD_DIM)
    angle = position.astype(jnp.float32)[:, None] * freq[None, :]
    cosine, sine = jnp.cos(angle), jnp.sin(angle)
    return jnp.concatenate([cosine, cosine], axis=-1), jnp.concatenate([-sine, sine], axis=-1)


def project_body(rotated, spot, x0, x1, x2, x3, w, cosine, sine, *rest):
    outs, held = rest[:-1], rest[-1]
    step = pl.program_id(0)
    for index, x in enumerate((x0, x1, x2, x3)):

        @pl.when(step == index)
        def _(x=x):
            held[...] = x[...]

    tile = 256

    def rows(r, carry):
        at = pl.ds(pl.multiple_of(r * tile, tile), tile)
        product = jnp.dot(held[at, :], w[...], preferred_element_type=jnp.float32)
        c, s = cosine[at, :], sine[at, :]
        column = 0
        for out in outs:
            for head in range(out.shape[1] // HEAD_DIM):
                part = product[:, column : column + HEAD_DIM]
                if column < rotated:
                    part = part * c + pltpu.roll(part, HEAD_DIM // 2, 1) * s
                out[at, head * HEAD_DIM : (head + 1) * HEAD_DIM] = part.astype(jnp.bfloat16)
                column += HEAD_DIM
        return carry

    lax.fori_loop(0, held.shape[0] // tile, rows, 0)


def project(spot, blocks, weights, half, cosine, sine, widths, rotated):
    rows, depth = blocks[0].shape
    columns = sum(widths)
    whole = pl.BlockSpec((rows, depth), lambda s, spot: (0, 0))
    table = pl.BlockSpec((rows, HEAD_DIM), lambda s, spot: (spot[s], 0))
    return pl.pallas_call(
        functools.partial(project_body, rotated),
        grid_spec=pltpu.PrefetchScalarGridSpec(
            num_scalar_prefetch=1,
            grid=(GROUP,),
            in_specs=[whole] * 4
            + [pl.BlockSpec((depth, columns), lambda s, spot: (0, half)), table, table],
            out_specs=[pl.BlockSpec((rows, width), lambda s, spot: (spot[s], 0)) for width in widths],
            scratch_shapes=[pltpu.VMEM((rows, depth), jnp.bfloat16)],
        ),
        out_shape=[jax.ShapeDtypeStruct((GROUP * rows, width), jnp.bfloat16) for width in widths],
        compiler_params=pltpu.CompilerParams(vmem_limit_bytes=VMEM),
        cost_estimate=pl.CostEstimate(
            flops=2 * GROUP * rows * depth * columns, bytes_accessed=GROUP * rows * (depth + columns) * 2, transcendentals=0
        ),
    )(spot, *blocks, weights, cosine, sine)


def attend_body(back, live, q, k_own, v_own, k_prev, v_prev, out, k_all, v_all):
    rows = q.shape[0]
    pages = rows // PAGE
    pad = CHUNK * PAGE
    wide = CHUNK * PAGE
    for buffer, prev, own in ((k_all, k_prev, k_own), (v_all, v_prev, v_own)):
        buffer[0:pad, :] = jnp.zeros((pad, KV_COLS), jnp.bfloat16)
        buffer[pad : pad + rows, :] = prev[...]
        buffer[pad + rows :, :] = own[...]
    factor = math.log2(math.e) / math.sqrt(HEAD_DIM)
    height = SHARE * PAGE
    row = lax.broadcasted_iota(jnp.int32, (height, wide), 0) % PAGE
    causal = lax.broadcasted_iota(jnp.int32, (height, wide), 1) - (wide - PAGE) <= row
    key_at = lax.broadcasted_iota(jnp.int32, (1, wide), 1)
    row_in = lax.broadcasted_iota(jnp.int32, (height, 1), 0) % PAGE

    def page_step(page, carry):
        reach = back[page]
        at = pl.ds(pl.multiple_of(page * PAGE, PAGE), PAGE)
        queries = [
            jnp.concatenate(
                [q[at, (h * SHARE + i) * HEAD_DIM : (h * SHARE + i + 1) * HEAD_DIM] for i in range(SHARE)], axis=0
            )
            for h in range(KV_PER)
        ]

        def chunk(index, state, diagonal):
            first = page + CHUNK + pages - (CHUNK - 1) - CHUNK * index
            where = pl.ds(pl.multiple_of(first * PAGE, PAGE), wide)
            low = (CHUNK - 1 + CHUNK * index - reach) * PAGE
            bias = jnp.where(key_at >= low, 0.0, NEG)
            fresh = []
            for h in range(KV_PER):
                keys = k_all[where, h * HEAD_DIM : (h + 1) * HEAD_DIM]
                values = v_all[where, h * HEAD_DIM : (h + 1) * HEAD_DIM]
                scores = lax.dot_general(
                    queries[h], keys, (((1,), (1,)), ((), ())), preferred_element_type=jnp.float32
                ) + bias
                if diagonal:
                    scores = jnp.where(causal, scores, NEG)
                best = jnp.max(scores, axis=1, keepdims=True)
                if not diagonal:
                    top, total, numer = state[h]
                    best = jnp.maximum(top, best)
                expo = jnp.exp2(scores * factor - best * factor)
                part = expo[:, 0:PAGE]
                for piece in range(1, CHUNK):
                    part = part + expo[:, piece * PAGE : (piece + 1) * PAGE]
                product = jnp.dot(expo.astype(jnp.bfloat16), values, preferred_element_type=jnp.float32)
                if not diagonal:
                    shrink = jnp.exp2(top * factor - best * factor)
                    part = total * shrink + part
                    product = numer * shrink + product
                fresh.append((best, part, product))
            return tuple(fresh)

        state = chunk(0, None, True)
        state = lax.fori_loop(1, reach // CHUNK + 1, lambda i, s: chunk(i, s, False), state)
        alive = row_in < live[page]
        for h in range(KV_PER):
            _, part, numer = state[h]
            total = jnp.sum(part, axis=1, keepdims=True)
            result = jnp.where(alive, numer / total, 0.0).astype(jnp.bfloat16)
            for i in range(SHARE):
                head = h * SHARE + i
                out[at, head * HEAD_DIM : (head + 1) * HEAD_DIM] = result[i * PAGE : (i + 1) * PAGE]
        return carry

    lax.fori_loop(0, pages, page_step, 0)


def attend(back, live, q, k_own, v_own, k_prev, v_prev):
    rows = q.shape[0]
    smem = pl.BlockSpec(memory_space=pltpu.SMEM)
    vmem = pl.BlockSpec(memory_space=pltpu.VMEM)
    span = 2 * rows + CHUNK * PAGE
    return pl.pallas_call(
        attend_body,
        in_specs=[smem, smem] + [vmem] * 5,
        out_specs=vmem,
        out_shape=jax.ShapeDtypeStruct(q.shape, jnp.bfloat16),
        scratch_shapes=[pltpu.VMEM((span, KV_COLS), jnp.bfloat16), pltpu.VMEM((span, KV_COLS), jnp.bfloat16)],
        compiler_params=pltpu.CompilerParams(vmem_limit_bytes=VMEM),
        cost_estimate=pl.CostEstimate(flops=12 * 10**9, bytes_accessed=8 * 2**20, transcendentals=10**7),
    )(back, live, q, k_own, v_own, k_prev, v_prev)


def pages_body(source, live, k, v, k_out, v_out):
    row = lax.broadcasted_iota(jnp.int32, (PAGE, 1), 0)

    def one(slot, carry):
        page = source[slot]
        at = pl.ds(pl.multiple_of(page * PAGE, PAGE), PAGE)
        keep = row < live[page]
        k_out[slot] = jnp.where(keep, k[at, :].astype(jnp.float32), 0.0).astype(jnp.bfloat16)
        v_out[slot] = jnp.where(keep, v[at, :].astype(jnp.float32), 0.0).astype(jnp.bfloat16)
        return carry

    lax.fori_loop(0, k_out.shape[0], one, 0)


def order_pages(source, live, k, v):
    smem = pl.BlockSpec(memory_space=pltpu.SMEM)
    vmem = pl.BlockSpec(memory_space=pltpu.VMEM)
    shape = jax.ShapeDtypeStruct((k.shape[0] // PAGE, PAGE, k.shape[1]), jnp.bfloat16)
    return pl.pallas_call(
        pages_body,
        in_specs=[smem, smem, vmem, vmem],
        out_specs=[vmem, vmem],
        out_shape=[shape, shape],
        compiler_params=pltpu.CompilerParams(vmem_limit_bytes=VMEM),
        cost_estimate=pl.CostEstimate(flops=10**6, bytes_accessed=4 * 2**20, transcendentals=0),
    )(source, live, k, v)


def output_body(a, w, out):
    depth = a.shape[2]
    total = jnp.dot(a[0], w[0:depth, :], preferred_element_type=jnp.float32)
    for index in range(1, a.shape[0]):
        total += jnp.dot(a[index], w[index * depth : (index + 1) * depth, :], preferred_element_type=jnp.float32)
    out[...] = total.astype(jnp.bfloat16)


def output(a, w):
    parts, rows, depth = a.shape
    columns, tile = w.shape[1], 256
    return pl.pallas_call(
        output_body,
        grid=(columns // tile,),
        in_specs=[
            pl.BlockSpec((parts, rows, depth), lambda n: (0, 0, 0)),
            pl.BlockSpec((parts * depth, tile), lambda n: (0, n)),
        ],
        out_specs=pl.BlockSpec((rows, tile), lambda n: (0, n)),
        out_shape=jax.ShapeDtypeStruct((rows, columns), jnp.bfloat16),
        compiler_params=pltpu.CompilerParams(vmem_limit_bytes=VMEM),
        cost_estimate=pl.CostEstimate(
            flops=2 * parts * rows * depth * columns, bytes_accessed=12 * 2**20, transcendentals=0
        ),
    )(a, w)


def shards(hidden_in, norm_gain, w_qk, w_v, w_o, prompt_pages, last_fill, page_slots):
    rows = hidden_in.shape[0]
    inside = ("c", "y")
    place = lax.axis_index("c") * 2 + lax.axis_index("y")
    pages = GROUP * rows // PAGE
    swap = [(0, 1), (1, 0)]

    width = HEADS * HEAD_DIM
    kv_width = KV_HEADS * HEAD_DIM
    depth = w_qk.shape[0]
    split = jnp.concatenate(
        [
            w_qk[:, width:].reshape(depth, GROUP, KV_COLS),
            w_v.reshape(depth, GROUP, KV_COLS),
            w_qk[:, :width].reshape(depth, GROUP, Q_COLS),
        ],
        axis=2,
    ).transpose(1, 0, 2)
    mine = lax.all_to_all(split, inside, split_axis=0, concat_axis=0, tiled=True)
    weights = lax.all_gather(mine.reshape(GROUP * depth, 2 * Q_COLS), "g", axis=0, tiled=True)

    normed = normalize(hidden_in, norm_gain)
    across = lax.ppermute(normed, "y", swap)
    core = lax.ppermute(normed, "c", swap)
    both = lax.ppermute(across, "c", swap)
    spot = jnp.arange(GROUP, dtype=jnp.int32) ^ place

    back, live = page_tables(lax.axis_index("g") * pages, pages, prompt_pages, last_fill)
    cosine, sine = rope_tables(back, pages)

    blocks = (normed, across, core, both)
    keys, values = project(spot, blocks, weights, 0, cosine, sine, (KV_COLS, KV_COLS), KV_COLS)
    groups = lax.axis_size("g")
    onward = [(i, i + 1) for i in range(groups - 1)]
    k_prev = lax.ppermute(keys, "g", onward)
    v_prev = lax.ppermute(values, "g", onward)
    (queries,) = project(spot, blocks, weights, 1, cosine, sine, (Q_COLS,), Q_COLS)

    slots = lax.all_gather(page_slots, "c", axis=0, tiled=False)
    order = jnp.arange(slots.shape[1], dtype=jnp.int32)
    hit = slots[:, None, :] == order[None, :, None]
    source = jnp.sum(jnp.where(hit, order[None, None, :], 0), axis=2)
    source = (source + jnp.arange(2, dtype=jnp.int32)[:, None] * slots.shape[1]).reshape(pages)
    k_pages, v_pages = order_pages(source.astype(jnp.int32), live, keys, values)
    key_cache = lax.all_to_all(k_pages, inside, split_axis=0, concat_axis=2, tiled=True)
    value_cache = lax.all_to_all(v_pages, inside, split_axis=0, concat_axis=2, tiled=True)

    w_out = lax.all_gather(w_o, ("g", "c", "y"), axis=0, tiled=True)
    attn = attend(back, live, queries, keys, values, k_prev, v_prev)
    own = lax.all_to_all(attn.reshape(GROUP, rows, Q_COLS), inside, split_axis=0, concat_axis=0, tiled=True)
    return (output(own, w_out), key_cache, value_cache)


def solution(mesh):
    fine = Mesh(mesh.devices.reshape(-1, 2, 2), ("g", "c", "y"))
    tokens = ("g", "c", "y")
    in_specs = (
        P(tokens, None),
        P(),
        P(tokens, None),
        P(tokens, None),
        P(tokens, None),
        P(),
        P(),
        P(("g", "c")),
    )
    out_specs = (P(tokens, None), P(tokens, None, None), P(tokens, None, None))
    return jax.shard_map(shards, mesh=fine, in_specs=in_specs, out_specs=out_specs, check_vma=False)
```

time: 614 us -> 283 us (0.46)
  the two profiles are of different devices: /device:TPU:13 before, /device:TPU:10 now
where the time goes in v1:
time: 283 us; the launch traced here: 281 us
  waiting for transfers between devices  136 us (48%)
  Pallas kernels  80.4 us (28%)
  starting transfers between devices  18.4 us (7%)
  between operations  14.9 us (5%)
  blocking collectives  14.3 us (5%)
  other arithmetic  8.99 us (3%)
  local copies, waits for them, and re-layouts  7.98 us (3%)
    ppermute x1, waiting for transfers between devices, shards(): across = lax.ppermute(normed, 'y', swap)  47 us
    ppermute x1, waiting for transfers between devices, shards(): v_prev = lax.ppermute(values, 'g', onward)  44.9 us
    pallas_call x1, Pallas kernels, attend(): pl.pallas_call(attend_body, in_specs=[smem, smem] + [vmem] * 5, out_specs...  40.3 us
    pallas_call x2, Pallas kernels, project(): pl.pallas_call(functools.partial(project_body, rotated), grid_spec=pltpu....  26.3 us
    all_to_all x1, waiting for transfers between devices, shards(): lax.all_to_all(attn.reshape(GROUP, rows, Q_COLS), inside, split_axis=0, c...  23.5 us
    all_to_all x1, blocking collectives, shards(): lax.all_to_all(split, inside, split_axis=0, concat_axis=0, tiled=True)  11.9 us
    all_gather x1, waiting for transfers between devices, shards(): lax.all_gather(mine.reshape(GROUP * depth, 2 * Q_COLS), 'g', axis=0, tile...  10.6 us
    pallas_call x1, Pallas kernels, output(): pl.pallas_call(output_body, grid=(columns // tile,), in_specs=[pl.BlockSp...  10.4 us
  transfers between devices with their start and end apart: 10, of which 6 were waited for; matrix products, arithmetic and copies ran while one was open for 5% of the time, Pallas kernels for 25%

profile of v1, /device:TPU:10, one launch (start us, length us, event | category | flops | bytes accessed | tf_op | source)
XLA Modules:
  0.0 281.0 jit_solution(11220101536599051204)
XLA Ops:
  8.2 1.1 slice.6
  10.3 11.9 %all_to_all.46 = bf16[4,64,1024]{2,1,0:T(8,128)(2,1)} all-to-all(bf16[4,64,1024]{2,1,0:T(8,128)(2,1)S(1)} %maximum_bitcast_fusion), channel_id=1, replica_groups=mesh['g'=8,'c'=2,'y'=2] {'c','y'}, dimensions={0} | all-to-all | bytes 1048576 | tf_op jit(solution)/shard_map/all_to_all | solution.py:267
  23.5 1.1 copy-done.2
  25.4 47.0 %collective-permute-done.x1 = bf16[512,2048]{1,0:T(8,128)(2,1)} collective-permute-done((bf16[512,2048]{1,0:T(8,128)(2,1)S(1)}, bf16[512,2048]{1,0:T(8,128)(2,1)}, u32[]{:S(2)}, u32[]{:S(2)}) %collective-permute-start) | collective-permute-done | bytes 2097184 | tf_op jit(solution)/shard_map/ppermute | solution.py:271
  74.1 2.4 all-reduce
  78.1 3.7 %fusion.3 = (f32[2048,64]{1,0:T(8,128)S(1)}, f32[2048,64]{1,0:T(8,128)S(1)}, f32[2048,64]{1,0:T(8,128)S(1)}) fusion(f32[64]{0:T(128)S(1)} %multiply_power_fusion, f32[2048]{0:T(1024)S(1)} %convert_bitcast_fusion), kind=kLoop, calls=%fused_computation.10 | loop fusion | flops 262144 | bytes 1581312 | tf_op jit(solution)/shard_map/neg | solution.py:53
  81.8 1.9 pad_maximum_fusion
  83.8 10.6 %all-gather.4.cloned.1.call-done.w = bf16[2048,1024]{1,0:T(8,128)(2,1)} async-done(((bf16[256,1024]{1,0:T(8,128)(2,1)}), bf16[2048,1024]{1,0:T(8,128)(2,1)}) %all-gather.4.cloned.1.call-update) | async-done | bytes 4194320 | tf_op jit(solution)/shard_map/all_gather | solution.py:268
  94.4 12.8 %shard_map.104 = (bf16[2048,256]{1,0:T(8,128)(2,1)}, bf16[2048,256]{1,0:T(8,128)(2,1)}) custom-call(s32[4]{0:T(128)} %iota_xor_fusion.spot, bf16[512,2048]{1,0:T(8,128)(2,1)} %copy-done, bf16[512,2048]{1,0:T(8,128)(2,1)} %collective-permute-done.x1, bf16[512,2048]{1,0:T(8,128)(2,1)} %collective-permute-done.1.x2, ...), custom_call_target="tpu_custom_call" | custom-call | flops 4294967296 | bytes 10485760 | tf_op jit(solution)/shard_map/pallas_call | solution.py:89
  107.2 4.1 %collective-permute-start.3 = (bf16[2048,256]{1,0:T(8,128)(2,1)}, bf16[2048,256]{1,0:T(8,128)(2,1)S(1)}, u32[]{:S(2)}, u32[]{:S(2)}) collective-permute-start(bf16[2048,256]{1,0:T(8,128)(2,1)} %get-tuple-element.7.k_own.k), channel_id=1, source_target_pairs={{0,4},{4,8},{8,12},{12,16},{16,20},{20,24},{24,28},{1,5},{5,9},{9,... | collective-permute-start | bytes 3145736 | tf_op jit(solution)/shard_map/ppermute | solution.py:283
  111.3 2.5 collective-permute-start.4
  115.1 3.4 %shard_map.107 = (bf16[16,128,256]{2,1,0:T(8,128)(2,1)}, bf16[16,128,256]{2,1,0:T(8,128)(2,1)}) custom-call(s32[16]{0:T(128)} %add.69.source, s32[16]{0:T(128)} %compare_select_fusion.live, bf16[2048,256]{1,0:T(8,128)(2,1)} %get-tuple-element.7.k_own.k, bf16[2048,256]{1,0:T(8,128)(2,1)} %get-tuple-element.8.v_own.v), custom_call_target="tpu_custom_call" | custom-call | flops 1000000 | bytes 4194304 | tf_op jit(solution)/shard_map/pallas_call | solution.py:212
  118.5 3.5 %all-to-all-start.2 = ((bf16[16,128,256]{2,1,0:T(8,128)(2,1)}), bf16[16,128,256]{2,1,0:T(8,128)(2,1)S(1)}, u32[]{:S(2)}, u32[]{:S(2)}) async-start(bf16[16,128,256]{2,1,0:T(8,128)(2,1)} %get-tuple-element.9), calls=%async_computation.2 | async-start | bytes 2097152 | tf_op jit(solution)/shard_map/all_to_all | solution.py:293
  122.0 13.5 %shard_map.103.q = bf16[2048,512]{1,0:T(8,128)(2,1)} custom-call(s32[4]{0:T(128)} %iota_xor_fusion.spot, bf16[512,2048]{1,0:T(8,128)(2,1)} %copy-done, bf16[512,2048]{1,0:T(8,128)(2,1)} %collective-permute-done.x1, bf16[512,2048]{1,0:T(8,128)(2,1)} %collective-permute-done.1.x2, bf16[512,2048]{1,0:T(8,128)(2,1)} %collective-permute-done.2.x3, ...), custom_call_target="tpu_custom_call" | custom-call | flops 4294967296 | bytes 10485760 | tf_op jit(solution)/shard_map/pallas_call | solution.py:89
  135.5 4.7 %all-to-all-done.2 = bf16[16,128,256]{2,1,0:T(8,128)(2,1)S(1)} async-done(((bf16[16,128,256]{2,1,0:T(8,128)(2,1)}), bf16[16,128,256]{2,1,0:T(8,128)(2,1)S(1)}, u32[]{:S(2)}, u32[]{:S(2)}) %all-to-all-start.2) | async-done | bytes 1048608 | tf_op jit(solution)/shard_map/all_to_all | solution.py:293
  140.2 3.5 %all-to-all-start.3 = ((bf16[16,128,256]{2,1,0:T(8,128)(2,1)}), bf16[16,128,256]{2,1,0:T(8,128)(2,1)S(1)}, u32[]{:S(2)}, u32[]{:S(2)}) async-start(bf16[16,128,256]{2,1,0:T(8,128)(2,1)} %get-tuple-element.10), calls=%async_computation.3 | async-start | bytes 2097152 | tf_op jit(solution)/shard_map/all_to_all | solution.py:294
  143.7 4.5 %collective-permute-done.3.k_prev = bf16[2048,256]{1,0:T(8,128)(2,1)S(1)} collective-permute-done((bf16[2048,256]{1,0:T(8,128)(2,1)}, bf16[2048,256]{1,0:T(8,128)(2,1)S(1)}, u32[]{:S(2)}, u32[]{:S(2)}) %collective-permute-start.3) | collective-permute-done | bytes 1048608 | tf_op jit(solution)/shard_map/ppermute | solution.py:283
  148.2 44.9 %collective-permute-done.4.v_prev = bf16[2048,256]{1,0:T(8,128)(2,1)} collective-permute-done((bf16[2048,256]{1,0:T(8,128)(2,1)}, bf16[2048,256]{1,0:T(8,128)(2,1)}, u32[]{:S(2)}, u32[]{:S(2)}) %collective-permute-start.4) | collective-permute-done | bytes 1048608 | tf_op jit(solution)/shard_map/ppermute | solution.py:284
  193.1 40.3 %shard_map.105 = bf16[2048,512]{1,0:T(8,128)(2,1)} custom-call(s32[16]{0:T(128)} %get-tuple-element.15.back, s32[16]{0:T(128)} %compare_select_fusion.live, bf16[2048,512]{1,0:T(8,128)(2,1)} %shard_map.103.q, bf16[2048,256]{1,0:T(8,128)(2,1)} %get-tuple-element.7.k_own.k, bf16[2048,256]{1,0:T(8,128)(2,1)} %get-tuple-element.8.v_own.v, ...), custom_call_target="tpu_custom_call" | custom-call | flops 12000000000 | bytes 8388608 | tf_op jit(solution)/shard_map/pallas_call | solution.py:183
  233.4 4.5 %all-to-all-start.1 = ((bf16[4,512,512]{2,1,0:T(8,128)(2,1)}), bf16[4,512,512]{2,1,0:T(8,128)(2,1)}, u32[]{:S(2)}, u32[]{:S(2)}) async-start(bf16[4,512,512]{2,1,0:T(8,128)(2,1)} %bitcast.30), calls=%async_computation.1 | async-start | bytes 4194304 | tf_op jit(solution)/shard_map/all_to_all | solution.py:298
  237.9 1.1 copy.32
  239.0 1.1 copy.33
  240.2 23.5 %all-to-all-done.1.a = bf16[4,512,512]{2,1,0:T(8,128)(2,1)} async-done(((bf16[4,512,512]{2,1,0:T(8,128)(2,1)}), bf16[4,512,512]{2,1,0:T(8,128)(2,1)}, u32[]{:S(2)}, u32[]{:S(2)}) %all-to-all-start.1) | async-done | bytes 2097184 | tf_op jit(solution)/shard_map/all_to_all | solution.py:298
  263.7 10.4 %shard_map.106 = bf16[512,2048]{1,0:T(8,128)(2,1)} custom-call(bf16[4,512,512]{2,1,0:T(8,128)(2,1)} %all-to-all-done.1.a, bf16[2048,2048]{1,0:T(8,128)(2,1)} %all-gather.6.cloned.1.call-done.w), custom_call_target="tpu_custom_call" | custom-call | flops 4294967296 | bytes 12582912 | tf_op jit(solution)/shard_map/pallas_call | solution.py:233
  (54 shorter events, 8.0 us)
Async XLA Ops:
  7.2 87.3 %all-gather.4.cloned.1.call-start = ((), (), s32[]{:S(2)}) async-start(), calls=%async_computation.4 | async-start | bytes 4718592 | tf_op jit(solution)/shard_map/all_gather | solution.py:268
  8.2 14.8 %copy-start.1 = (bf16[512,2048]{1,0:T(8,128)(2,1)S(1)}, bf16[512,2048]{1,0:T(8,128)(2,1)}, u32[]{:S(2)}) copy-start(bf16[512,2048]{1,0:T(8,128)(2,1)} %param.8) | copy-start | bytes 6291460
  10.3 13.2 %copy-start.3 = (f32[2048]{0:T(1024)S(1)}, f32[2048]{0:T(1024)}, u32[]{:S(2)}) copy-start(f32[2048]{0:T(1024)} %param.9) | copy-start | bytes 24580
  22.3 241.4 %all-gather.6.cloned.1.call-start = ((), (), s32[]{:S(2)}) async-start(), calls=%async_computation.5 | async-start | bytes 8650752 | tf_op jit(solution)/shard_map/all_gather | solution.py:296
  23.0 1.6 copy-start.2
  24.6 47.8 %copy-start.4 = (s32[16]{0:T(128)S(1)}, s32[16]{0:T(128)}, u32[]{:S(2)}) copy-start(s32[16]{0:T(128)} %param.13) | copy-start | bytes 196
  24.6 48.0 %copy-start.8 = (u32[32]{0:T(128)S(1)}, u32[32]{0:T(128)}, u32[]{:S(2)}) copy-start(u32[32]{0:T(128)} %constant.46) | copy-start | bytes 388
  24.6 49.3 %copy-start.7 = (s32[8]{0:T(128)S(1)}, s32[8]{0:T(128)}, u32[]{:S(2)}) copy-start(s32[8]{0:T(128)} %param.15) | copy-start | bytes 100
  24.6 52.7 %copy-start.5 = (s32[16]{0:T(128)S(1)}, s32[16]{0:T(128)}, u32[]{:S(2)}) copy-start(s32[16]{0:T(128)} %param.14) | copy-start | bytes 196
  25.2 58.6 %copy-start = (bf16[512,2048]{1,0:T(8,128)(2,1)}, bf16[512,2048]{1,0:T(8,128)(2,1)S(1)}, u32[]{:S(2)}) copy-start(bf16[512,2048]{1,0:T(8,128)(2,1)S(1)} %fusion.2.x0) | copy-start | bytes 6291460
  25.2 47.2 %collective-permute-start = (bf16[512,2048]{1,0:T(8,128)(2,1)S(1)}, bf16[512,2048]{1,0:T(8,128)(2,1)}, u32[]{:S(2)}, u32[]{:S(2)}) collective-permute-start(bf16[512,2048]{1,0:T(8,128)(2,1)S(1)} %fusion.2.x0), channel_id=1, source_target_pairs={{0,1},{1,0},{2,3},{3,2},{4,5},{5,4},{6,7},{7,6},{8,9},{9,8},{10,11... | collective-permute-start | bytes 6291464 | tf_op jit(solution)/shard_map/ppermute | solution.py:271
  25.4 58.4 %collective-permute-start.1 = (bf16[512,2048]{1,0:T(8,128)(2,1)S(1)}, bf16[512,2048]{1,0:T(8,128)(2,1)}, u32[]{:S(2)}, u32[]{:S(2)}) collective-permute-start(bf16[512,2048]{1,0:T(8,128)(2,1)S(1)} %fusion.2.x0), channel_id=1, source_target_pairs={{0,2},{2,0},{1,3},{3,1},{4,6},{6,4},{5,7},{7,5},{8,10},{10,8},{9,1... | collective-permute-start | bytes 6291464 | tf_op jit(solution)/shard_map/ppermute | solution.py:272
  72.4 11.4 %collective-permute-start.2 = (bf16[512,2048]{1,0:T(8,128)(2,1)}, bf16[512,2048]{1,0:T(8,128)(2,1)}, u32[]{:S(2)}, u32[]{:S(2)}) collective-permute-start(bf16[512,2048]{1,0:T(8,128)(2,1)} %collective-permute-done.x1), channel_id=1, source_target_pairs={{0,2},{2,0},{1,3},{3,1},{4,6},{6,4},{5,7},{7,5},{8,10},{10,8},{9,1... | collective-permute-start | bytes 6291464 | tf_op jit(solution)/shard_map/ppermute | solution.py:273
  107.2 41.0 %collective-permute-start.3 = (bf16[2048,256]{1,0:T(8,128)(2,1)}, bf16[2048,256]{1,0:T(8,128)(2,1)S(1)}, u32[]{:S(2)}, u32[]{:S(2)}) collective-permute-start(bf16[2048,256]{1,0:T(8,128)(2,1)} %get-tuple-element.7.k_own.k), channel_id=1, source_target_pairs={{0,4},{4,8},{8,12},{12,16},{16,20},{20,24},{24,28},{1,5},{5,9},{9,... | collective-permute-start | bytes 3145736 | tf_op jit(solution)/shard_map/ppermute | solution.py:283
  111.3 81.8 %collective-permute-start.4 = (bf16[2048,256]{1,0:T(8,128)(2,1)}, bf16[2048,256]{1,0:T(8,128)(2,1)}, u32[]{:S(2)}, u32[]{:S(2)}) collective-permute-start(bf16[2048,256]{1,0:T(8,128)(2,1)} %get-tuple-element.8.v_own.v), channel_id=1, source_target_pairs={{0,4},{4,8},{8,12},{12,16},{16,20},{20,24},{24,28},{1,5},{5,9},{9,... | collective-permute-start | bytes 3145736 | tf_op jit(solution)/shard_map/ppermute | solution.py:284
  118.5 21.7 %all-to-all-start.2 = ((bf16[16,128,256]{2,1,0:T(8,128)(2,1)}), bf16[16,128,256]{2,1,0:T(8,128)(2,1)S(1)}, u32[]{:S(2)}, u32[]{:S(2)}) async-start(bf16[16,128,256]{2,1,0:T(8,128)(2,1)} %get-tuple-element.9), calls=%async_computation.2 | async-start | bytes 2097152 | tf_op jit(solution)/shard_map/all_to_all | solution.py:293
  140.2 93.2 %all-to-all-start.3 = ((bf16[16,128,256]{2,1,0:T(8,128)(2,1)}), bf16[16,128,256]{2,1,0:T(8,128)(2,1)S(1)}, u32[]{:S(2)}, u32[]{:S(2)}) async-start(bf16[16,128,256]{2,1,0:T(8,128)(2,1)} %get-tuple-element.10), calls=%async_computation.3 | async-start | bytes 2097152 | tf_op jit(solution)/shard_map/all_to_all | solution.py:294
  148.2 44.9 %copy-start.6 = (bf16[2048,256]{1,0:T(8,128)(2,1)}, bf16[2048,256]{1,0:T(8,128)(2,1)S(1)}, u32[]{:S(2)}) copy-start(bf16[2048,256]{1,0:T(8,128)(2,1)S(1)} %collective-permute-done.3.k_prev) | copy-start | bytes 3145732
  233.4 30.3 %all-to-all-start.1 = ((bf16[4,512,512]{2,1,0:T(8,128)(2,1)}), bf16[4,512,512]{2,1,0:T(8,128)(2,1)}, u32[]{:S(2)}, u32[]{:S(2)}) async-start(bf16[4,512,512]{2,1,0:T(8,128)(2,1)} %bitcast.30), calls=%async_computation.1 | async-start | bytes 4194304 | tf_op jit(solution)/shard_map/all_to_all | solution.py:298
Sparse Core Ops, SparseCore 0:
  22.4 71.9 all-gather.3
  97.5 98.4 all-gather.5
